TPU v7x, 256 devices: a whole 4x4x8 slice. The times are simulated.
256 devices in a mesh: chan: 4 (over y), ctx: 64 (over z, x, core).
Axes of the slice: x: 4, y: 4, z: 8, core: 2. Of those that a mesh axis runs over, the one named last changes fastest.
Arguments:
- streams: bfloat16 [3, 8192, 8192], P(None, 'ctx', 'chan'), may hold values from -6 to 6
- short_filter: float32 [3, 3, 8192], P(None, None, 'chan'), may hold values from -3 to 3
- rates: float32 [16, 8192], P(None, 'chan'), may hold values from 6.1035156e-05 to 0.03
- residues: float32 [16, 8192], P(None, 'chan'), may hold values from -0.03 to 0.03
- skip: float32 [8192], P('chan'), may hold values from 0.5 to 1.5
Outputs:
- mixed: bfloat16 [8192, 8192], P('ctx', 'chan')
All inputs are finite; a program needn't handle non-finite values.
Results may differ from a plain program's by a relative error of at most 0.009.
Values may be sent and summed in bfloat16 or wider, within the bound.
A program may use at most 128 MiB of HBM per device.

v0:
```python
import jax
import jax.numpy as jnp
from jax import lax
from jax.experimental import pallas as pl
from jax.experimental.pallas import tpu as pltpu
from jax.sharding import PartitionSpec as P

MESH = pl.DeviceIdType.MESH
LANES = 128
SUB = 8
GROUP = 8
F32 = jnp.float32
BF16 = jnp.bfloat16


def lanes(index, width=LANES):
    return pl.ds(pl.multiple_of(index * width, width), width)


def gather_rows(rows):
    steps = rows // SUB
    r = lax.broadcasted_iota(jnp.int32, (rows + 2 * SUB, rows), 0)
    t = lax.broadcasted_iota(jnp.int32, (rows + 2 * SUB, rows), 1)
    return (t == (r & (SUB - 1)) * steps + (r >> 3) - 2).astype(F32).astype(BF16)


def scatter_rows(rows):
    steps = rows // SUB
    t = lax.broadcasted_iota(jnp.int32, (rows, rows), 0)
    r = lax.broadcasted_iota(jnp.int32, (rows, rows), 1)
    return (t == (r & (SUB - 1)) * steps + (r >> 3)).astype(F32).astype(BF16)


def featurize(perm, streams, taps, stream, at):
    x = jnp.dot(perm, streams[stream, :, at], preferred_element_type=F32)
    rows = x.shape[0] - 2 * SUB
    return (
        taps[0, pl.ds(stream, 1), at] * x[2 * SUB :]
        + taps[1, pl.ds(stream, 1), at] * x[SUB : SUB + rows]
        + taps[2, pl.ds(stream, 1), at] * x[:rows]
    )


def edge_terms(taps, stream, at, old, older):
    one = taps[1, pl.ds(stream, 1), at]
    two = taps[2, pl.ds(stream, 1), at]
    return one * old + two * older, two * old


def first_kernel(
    streams_hbm,
    taps_hbm,
    rates_hbm,
    residues_hbm,
    skip_hbm,
    base,
    gate,
    inner,
    reach,
    state,
    decay,
    streams,
    taps,
    rates,
    residues,
    skip,
    sig,
    heads,
    halo_out,
    halo_in,
    sbuf,
    abuf,
    tbuf,
    bbuf,
    hbuf,
    cbuf,
    load_sem,
    halo_sem,
    a_send,
    a_recv,
    b_send,
    b_recv,
    c_send,
    c_recv,
):
    rows, width = sig.shape
    steps = rows // SUB
    modes = rates.shape[0]
    tiles = width // LANES
    piece = width // GROUP
    me = lax.axis_index("ctx")
    count = lax.axis_size("ctx")
    outer = count // GROUP
    g = me // GROUP
    l = me - g * GROUP

    loads = [
        pltpu.make_async_copy(streams_hbm.at[1], streams.at[1], load_sem.at[0]),
        pltpu.make_async_copy(streams_hbm.at[2], streams.at[2], load_sem.at[1]),
        pltpu.make_async_copy(taps_hbm, taps, load_sem.at[2]),
        pltpu.make_async_copy(rates_hbm, rates, load_sem.at[3]),
        pltpu.make_async_copy(streams_hbm.at[0], streams.at[0], load_sem.at[4]),
        pltpu.make_async_copy(residues_hbm, residues, load_sem.at[5]),
        pltpu.make_async_copy(skip_hbm, skip, load_sem.at[6]),
    ]
    for load in loads:
        load.start()

    bar = pltpu.get_barrier_semaphore()
    for k in range(1, GROUP):
        pl.semaphore_signal(
            bar, inc=1, device_id={"ctx": g * GROUP + lax.rem(l + k, GROUP)}, device_id_type=MESH
        )
    for k in range(1, outer):
        pl.semaphore_signal(
            bar, inc=1, device_id={"ctx": lax.rem(g + k, outer) * GROUP + l}, device_id_type=MESH
        )
    pl.semaphore_signal(bar, inc=1, device_id={"ctx": lax.rem(me + 1, count)}, device_id_type=MESH)
    pl.semaphore_signal(
        bar, inc=1, device_id={"ctx": lax.rem(me + count - 1, count)}, device_id_type=MESH
    )

    perm = gather_rows(rows)
    for load in loads[:3]:
        load.wait()

    def signal_step(c, carry):
        at = lanes(c, 2 * LANES)
        one = featurize(perm, streams, taps, 1, at)
        two = featurize(perm, streams, taps, 2, at)
        sig[:, at] = one * two
        heads[0:1, at] = one[0:1]
        heads[1:2, at] = one[SUB : SUB + 1]
        heads[2:3, at] = two[0:1]
        heads[3:4, at] = two[SUB : SUB + 1]
        return carry

    lax.fori_loop(0, tiles // 2, signal_step, 0)

    loads[4].wait()
    for s in range(3):
        tail = streams[s, pl.ds(rows - 16, 16), :].astype(F32)
        halo_out[2 * s : 2 * s + 2, :] = tail[14:16]

    pl.semaphore_wait(bar, GROUP - 1 + outer - 1 + 2)
    halo = pltpu.make_async_remote_copy(
        src_ref=halo_out,
        dst_ref=halo_in,
        send_sem=halo_sem.at[0],
        recv_sem=halo_sem.at[1],
        device_id={"ctx": lax.rem(me + 1, count)},
        device_id_type=MESH,
    )

    @pl.when(me < count - 1)
    def _():
        halo.start()

    loads[3].wait()
    decay[...] = jnp.exp(-rates[...])

    sub_row = lax.broadcasted_iota(jnp.int32, (SUB, LANES), 0).astype(F32)
    to_end = (SUB - 1 - sub_row) * (-float(steps))

    def state_step(p, carry):
        for half in range(piece // LANES):
            at = lanes(p * (piece // LANES) + half)
            factor = [
                jnp.broadcast_to(decay[pl.ds(m, 1), at], (SUB, LANES)) for m in range(modes)
            ]
            held = [sig[0:SUB, at]] * modes
            for b in range(1, steps):
                x = sig[SUB * b : SUB * b + SUB, at]
                held = [h * f + x for h, f in zip(held, factor)]
            ends = []
            for m in range(modes):
                weight = jnp.exp(to_end * rates[pl.ds(m, 1), at])
                ends.append(jnp.sum(held[m] * weight, axis=0, keepdims=True))
            sbuf[p, :, half * LANES : half * LANES + LANES] = jnp.concatenate(ends, axis=0)
        return carry

    lax.fori_loop(0, GROUP, state_step, 0)

    @pl.when(me > 0)
    def _():
        halo.wait_recv()

    @pl.when(me == 0)
    def _():
        halo_in[...] = jnp.zeros_like(halo_in)

    def edge_step(p, carry):
        at = lanes(p, piece)
        one0, one1 = edge_terms(taps, 1, at, halo_in[3:4, at], halo_in[2:3, at])
        two0, two1 = edge_terms(taps, 2, at, halo_in[5:6, at], halo_in[4:5, at])
        new0 = (heads[0:1, at] + one0) * (heads[2:3, at] + two0)
        new1 = (heads[1:2, at] + one1) * (heads[3:4, at] + two1)
        add0 = new0 - sig[0:1, at]
        add1 = new1 - sig[SUB : SUB + 1, at]
        sig[0:1, at] = new0
        sig[SUB : SUB + 1, at] = new1
        rate = rates[:, at]
        sbuf[p] += jnp.exp(rate * (1.0 - rows)) * add0 + jnp.exp(rate * (2.0 - rows)) * add1
        return carry

    lax.fori_loop(0, GROUP, edge_step, 0)

    abuf[l] = sbuf[l]
    for k in range(1, GROUP):
        to = lax.rem(l + k, GROUP)
        pltpu.make_async_remote_copy(
            src_ref=sbuf.at[to],
            dst_ref=abuf.at[l],
            send_sem=a_send,
            recv_sem=a_recv,
            device_id={"ctx": g * GROUP + to},
            device_id_type=MESH,
        ).start()

    def gate_step(c, carry):
        at = lanes(c, 2 * LANES)
        gate[:, at] = featurize(perm, streams, taps, 0, at)
        zero0, zero1 = edge_terms(taps, 0, at, halo_in[1:2, at], halo_in[0:1, at])
        gate[0:1, at] += zero0
        gate[SUB : SUB + 1, at] += zero1
        return carry

    lax.fori_loop(0, tiles // 2, gate_step, 0)
    loads[5].wait()
    loads[6].wait()

    def own_step(c, carry):
        at = lanes(c)
        factor = [jnp.broadcast_to(decay[pl.ds(m, 1), at], (SUB, LANES)) for m in range(modes)]
        weight = [jnp.broadcast_to(residues[pl.ds(m, 1), at], (SUB, LANES)) for m in range(modes)]
        direct = jnp.broadcast_to(skip[0:1, at], (SUB, LANES))
        held = None
        for b in range(steps):
            x = sig[SUB * b : SUB * b + SUB, at]
            held = [x] * modes if b == 0 else [h * f + x for h, f in zip(held, factor)]
            total = direct * x
            for h, w in zip(held, weight):
                total = total + h * w
            base[SUB * b : SUB * b + SUB, at] = total
        for m in range(modes):
            rate = rates[pl.ds(m, 1), at]
            lead = weight[m] * factor[m]
            begin = jnp.where(sub_row < 1, 0.0, pltpu.roll(held[m], 1, 0))
            for reach_rows in (1, 2, 4):
                power = jnp.exp(rate * (-float(steps * reach_rows)))
                begin = begin + power * jnp.where(
                    sub_row < reach_rows, 0.0, pltpu.roll(begin, reach_rows, 0)
                )
            inner[c, m] = lead * begin
            reach[c, m] = lead * jnp.exp(sub_row * (rate * (-float(steps))))
        return carry

    lax.fori_loop(0, tiles // 4, own_step, 0)

    mine = lanes(l, piece)
    chunk_decay = jnp.exp(rates[:, mine] * (-float(rows)))
    group_decay = jnp.exp(rates[:, mine] * (-float(rows * GROUP)))
    others = pl.ds(0, GROUP - 1)
    pltpu.make_async_copy(sbuf.at[others], abuf.at[others], a_recv).wait()
    total = abuf[0]
    for k in range(1, GROUP):
        total = total * chunk_decay + abuf[k]
    tbuf[...] = total

    def group_copy(k):
        return pltpu.make_async_remote_copy(
            src_ref=tbuf,
            dst_ref=bbuf.at[g],
            send_sem=b_send.at[k],
            recv_sem=b_recv.at[g],
            device_id={"ctx": lax.rem(g + k, outer) * GROUP + l},
            device_id_type=MESH,
        )

    for k in range(1, outer):

        @pl.when(g + k < outer)
        def _():
            group_copy(k).start()

    lax.fori_loop(tiles // 4, 3 * tiles // 4, own_step, 0)

    hbuf[0] = jnp.zeros_like(total)
    for k in range(outer - 1):

        @pl.when(k < g)
        def _():
            pltpu.make_async_copy(tbuf, bbuf.at[k], b_recv.at[k]).wait()
            hbuf[0] = hbuf[0] * group_decay + bbuf[k]

    held = hbuf[0]
    for k in range(1, GROUP):
        held = held * chunk_decay + abuf[k - 1]
        hbuf[k] = held

    cbuf[l] = hbuf[l]
    for k in range(1, GROUP):
        to = lax.rem(l + k, GROUP)
        pltpu.make_async_remote_copy(
            src_ref=hbuf.at[to],
            dst_ref=cbuf.at[l],
            send_sem=c_send,
            recv_sem=c_recv,
            device_id={"ctx": g * GROUP + to},
            device_id_type=MESH,
        ).start()

    lax.fori_loop(3 * tiles // 4, tiles, own_step, 0)

    @pl.when(me < count - 1)
    def _():
        halo.wait_send()

    pltpu.make_async_copy(sbuf.at[others], abuf.at[others], a_send).wait()
    for k in range(1, outer):

        @pl.when(g + k < outer)
        def _():
            group_copy(k).wait_send()

    pltpu.make_async_copy(hbuf.at[others], cbuf.at[others], c_recv).wait()
    state[...] = cbuf[...]
    pltpu.make_async_copy(hbuf.at[others], cbuf.at[others], c_send).wait()


def second_kernel(base, gate, inner, reach, state, decay, out_hbm, out, out_sem):
    rows, width = out.shape
    steps = rows // SUB
    modes = decay.shape[0]
    tiles = width // LANES
    piece = width // GROUP
    parts = 4
    back = scatter_rows(rows)

    def tile_step(p, carry):
        for half in range(piece // LANES):
            c = p * (piece // LANES) + half
            at = lanes(c)
            factor = [
                jnp.broadcast_to(decay[pl.ds(m, 1), at], (SUB, LANES)) for m in range(modes)
            ]
            term = [
                inner[c, m]
                + reach[c, m] * state[p, pl.ds(m, 1), half * LANES : half * LANES + LANES]
                for m in range(modes)
            ]
            mixed = []
            for b in range(steps):
                total = base[SUB * b : SUB * b + SUB, at]
                for h in term:
                    total = total + h
                mixed.append((gate[SUB * b : SUB * b + SUB, at] * total).astype(F32))
                if b < steps - 1:
                    term = [h * f for h, f in zip(term, factor)]
            mixed = jnp.concatenate(mixed, axis=0).astype(BF16)
            out[:, at] = jnp.dot(back, mixed, preferred_element_type=F32).astype(BF16)
        return carry

    copies = []
    for q in range(parts):
        lax.fori_loop(q * GROUP // parts, (q + 1) * GROUP // parts, tile_step, 0)
        at = pl.ds(q * width // parts, width // parts)
        copies.append(pltpu.make_async_copy(out.at[:, at], out_hbm.at[:, at], out_sem.at[q]))
        copies[-1].start()
    for copy in copies:
        copy.wait()


def local(streams, short_filter, rates, residues, skip):
    _, rows, width = streams.shape
    modes = rates.shape[0]
    tiles = width // LANES
    piece = width // GROUP
    outer = lax.axis_size("ctx") // GROUP
    steps = rows // SUB
    any_spec = pl.BlockSpec(memory_space=pl.ANY)
    hbm_spec = pl.BlockSpec(memory_space=pltpu.HBM)
    vmem_spec = pl.BlockSpec(memory_space=pltpu.VMEM)
    pieces = pltpu.VMEM((GROUP, modes, piece), F32)
    parts = pl.pallas_call(
        first_kernel,
        out_shape=[
            pltpu.VMEM((rows, width), F32),
            pltpu.VMEM((rows, width), F32),
            pltpu.VMEM((tiles, modes, SUB, LANES), F32),
            pltpu.VMEM((tiles, modes, SUB, LANES), F32),
            pltpu.VMEM((GROUP, modes, piece), F32),
            pltpu.VMEM((modes, width), F32),
        ],
        in_specs=[hbm_spec] * 5,
        out_specs=[vmem_spec] * 6,
        scratch_shapes=[
            pltpu.VMEM(streams.shape, BF16),
            pltpu.VMEM(short_filter.shape, F32),
            pltpu.VMEM(rates.shape, F32),
            pltpu.VMEM(rates.shape, F32),
            pltpu.VMEM((1, width), F32),
            pltpu.VMEM((rows, width), F32),
            pltpu.VMEM((4, width), F32),
            pltpu.VMEM((8, width), F32),
            pltpu.VMEM((8, width), F32),
            pieces,
            pieces,
            pltpu.VMEM((modes, piece), F32),
            pltpu.VMEM((outer, modes, piece), F32),
            pieces,
            pieces,
            pltpu.SemaphoreType.DMA((7,)),
            pltpu.SemaphoreType.DMA((2,)),
            pltpu.SemaphoreType.DMA,
            pltpu.SemaphoreType.DMA,
            pltpu.SemaphoreType.DMA((outer,)),
            pltpu.SemaphoreType.DMA((outer,)),
            pltpu.SemaphoreType.DMA,
            pltpu.SemaphoreType.DMA,
        ],
        compiler_params=pltpu.CompilerParams(
            collective_id=0, has_side_effects=True, vmem_limit_bytes=24 * 1024 * 1024
        ),
        name="chunk_state",
    )(streams, short_filter, rates, residues, skip[None, :])
    return pl.pallas_call(
        second_kernel,
        out_shape=jax.ShapeDtypeStruct((rows, width), BF16),
        in_specs=[vmem_spec] * 6,
        out_specs=any_spec,
        scratch_shapes=[pltpu.VMEM((rows, width), BF16), pltpu.SemaphoreType.DMA((4,))],
        compiler_params=pltpu.CompilerParams(vmem_limit_bytes=24 * 1024 * 1024),
        name="mix",
    )(*parts)


def solution(mesh):
    placed = (
        P(None, "ctx", "chan"),
        P(None, None, "chan"),
        P(None, "chan"),
        P(None, "chan"),
        P("chan"),
    )
    return jax.shard_map(
        local, mesh=mesh, in_specs=placed, out_specs=P("ctx", "chan"), check_vma=False
    )
```

profile of v0, /device:TPU:209, one launch (start us, length us, event | category | flops | bytes accessed | tf_op | source)
XLA Modules:
  0.0 30.8 jit_solution(12732498030267732814)
XLA Ops:
  0.0 0.0 copy-start
  0.0 1.4 %copy-done = bf16[3,128,2048]{2,1,0:T(8,128)(2,1)S(1)} copy-done((bf16[3,128,2048]{2,1,0:T(8,128)(2,1)S(1)}, bf16[3,128,2048]{2,1,0:T(8,128)(2,1)}, u32[]{:S(2)}) %copy-start) | copy-done | bytes 1572888
  1.4 0.0 copy-start.1
  1.4 0.9 %copy-done.1 = f32[16,2048]{1,0:T(8,128)S(1)} copy-done((f32[16,2048]{1,0:T(8,128)S(1)}, f32[16,2048]{1,0:T(8,128)}, u32[]{:S(2)}) %copy-start.1) | copy-done | bytes 131096
  2.3 0.0 copy-start.2
  2.3 0.9 %copy-done.2 = f32[16,2048]{1,0:T(8,128)S(1)} copy-done((f32[16,2048]{1,0:T(8,128)S(1)}, f32[16,2048]{1,0:T(8,128)}, u32[]{:S(2)}) %copy-start.2) | copy-done | bytes 131096
  3.2 0.0 copy-start.3
  3.2 0.9 %copy-done.3 = f32[3,3,2048]{2,1,0:T(4,128)S(1)} copy-done((f32[3,3,2048]{2,1,0:T(4,128)S(1)}, f32[3,3,2048]{2,1,0:T(4,128)}, u32[]{:S(2)}) %copy-start.3) | copy-done | bytes 73752
  4.1 0.0 copy-start.4
  4.1 0.7 %copy-done.4 = f32[2048]{0:T(1024)S(1)} copy-done((f32[2048]{0:T(1024)S(1)}, f32[2048]{0:T(1024)}, u32[]{:S(2)}) %copy-start.4) | copy-done | bytes 8216
  4.8 22.9 %chunk_state.1 = (f32[128,2048]{1,0:T(8,128)S(1)}, f32[128,2048]{1,0:T(8,128)S(1)}, f32[16,16,8,128]{3,2,1,0:T(8,128)S(1)}, f32[16,16,8,128]{3,2,1,0:T(8,128)S(1...) custom-call(bf16[3,128,2048]{2,1,0:T(8,128)(2,1)S(1)} %copy-done, f32[3,3,2048]{2,1,0:T(4,128)S(1)} %copy-done.3, ...), custom_call_target="tpu_custom_call" | custom-call | tf_op jit(solution)/shard_map/chunk_state/pallas_call | solution.py:385
  27.7 3.1 %mix.1 = bf16[128,2048]{1,0:T(8,128)(2,1)} custom-call(f32[128,2048]{1,0:T(8,128)S(1)} %get-tuple-element.11.base, f32[128,2048]{1,0:T(8,128)S(1)} %get-tuple-element.12.gate, f32[16,16,8,128]{3,2,1,0:T(8,128)S(1)} %get-tuple-element.13.inner, f32[16,16,8,128]{3,2,1,0:T(8,128)S(1)} %get-tuple-element.14.reach, f32[8,16,256]{2,1,0:T(8,128)S(1)} %get-tuple-element.15.state, ...), custom_call_target="tpu_custom_call" | custom-call | tf_op jit(solution)/shard_map/mix/pallas_call | solution.py:427
Async XLA Ops:
  0.0 1.4 %copy-start = (bf16[3,128,2048]{2,1,0:T(8,128)(2,1)S(1)}, bf16[3,128,2048]{2,1,0:T(8,128)(2,1)}, u32[]{:S(2)}) copy-start(bf16[3,128,2048]{2,1,0:T(8,128)(2,1)} %streams_hbm.1) | copy-start | bytes 4718596
  1.4 0.9 %copy-start.1 = (f32[16,2048]{1,0:T(8,128)S(1)}, f32[16,2048]{1,0:T(8,128)}, u32[]{:S(2)}) copy-start(f32[16,2048]{1,0:T(8,128)} %rates_hbm.1) | copy-start | bytes 393220
  2.3 0.9 %copy-start.2 = (f32[16,2048]{1,0:T(8,128)S(1)}, f32[16,2048]{1,0:T(8,128)}, u32[]{:S(2)}) copy-start(f32[16,2048]{1,0:T(8,128)} %residues_hbm.1) | copy-start | bytes 393220
  3.2 0.9 %copy-start.3 = (f32[3,3,2048]{2,1,0:T(4,128)S(1)}, f32[3,3,2048]{2,1,0:T(4,128)}, u32[]{:S(2)}) copy-start(f32[3,3,2048]{2,1,0:T(4,128)} %taps_hbm.1) | copy-start | bytes 221188
  4.1 0.7 %copy-start.4 = (f32[2048]{0:T(1024)S(1)}, f32[2048]{0:T(1024)}, u32[]{:S(2)}) copy-start(f32[2048]{0:T(1024)} %param.9) | copy-start | bytes 24580
where the time goes:
time: 31 us; the launch traced here: 30.8 us
  Pallas kernels  26 us (84%)
  local copies, waits for them, and re-layouts  4.8 us (15%)
    pallas_call x1, Pallas kernels, local(): pl.pallas_call(first_kernel, out_shape=[pltpu.VMEM((rows, width), F32), p...  22.9 us
    unnamed x10, local copies, waits for them, and re-layouts  4.8 us
    pallas_call x1, Pallas kernels, local(): pl.pallas_call(second_kernel, out_shape=jax.ShapeDtypeStruct((rows, width...  3.15 us

commit v1 on v0

v1 whole, which is shorter than its diff:
```python
import jax
import jax.numpy as jnp
from jax import lax
from jax.experimental import pallas as pl
from jax.experimental.pallas import tpu as pltpu
from jax.sharding import PartitionSpec as P

MESH = pl.DeviceIdType.MESH
LANES = 128
SUB = 8
GROUP = 8
CHIPS = GROUP // 2
F32 = jnp.float32
BF16 = jnp.bfloat16


def lanes(index, width=LANES):
    return pl.ds(pl.multiple_of(index * width, width), width)


def gather_rows(rows):
    steps = rows // SUB
    r = lax.broadcasted_iota(jnp.int32, (rows + 3 * SUB, rows), 0)
    t = lax.broadcasted_iota(jnp.int32, (rows + 3 * SUB, rows), 1)
    body = (r & (SUB - 1)) * steps + (r >> 3) - 2
    edge = (r & 3) + jnp.where((r & 3) < 2, 0, rows - 4)
    return (t == jnp.where(r < rows + 2 * SUB, body, edge)).astype(F32).astype(BF16)


def scatter_rows(rows):
    steps = rows // SUB
    t = lax.broadcasted_iota(jnp.int32, (rows, rows), 0)
    r = lax.broadcasted_iota(jnp.int32, (rows, rows), 1)
    return (t == (r & (SUB - 1)) * steps + (r >> 3)).astype(F32).astype(BF16)


def featurize(perm, streams, taps, stream, at):
    x = jnp.dot(perm, streams[stream, :, at], preferred_element_type=F32)
    rows = x.shape[0] - 3 * SUB
    features = (
        taps[0, pl.ds(stream, 1), at] * x[2 * SUB : 2 * SUB + rows]
        + taps[1, pl.ds(stream, 1), at] * x[SUB : SUB + rows]
        + taps[2, pl.ds(stream, 1), at] * x[:rows]
    )
    return features, x[2 * SUB + rows :]


def edge_features(weights, own, before):
    row = lax.broadcasted_iota(jnp.int32, own.shape, 0)
    one_back = jnp.where((row & 1) == 0, pltpu.roll(before, 5, 0), pltpu.roll(own, 1, 0))
    return weights[0] * own + weights[1] * one_back + weights[2] * pltpu.roll(before, 6, 0)


def edge_signal(weights, own, before):
    features = edge_features(weights, own, before)
    return features * pltpu.roll(features, 4, 0)


def edge_weights(taps, at):
    row = lax.broadcasted_iota(jnp.int32, (SUB, LANES), 0)
    return [jnp.where(row < 4, taps[j, 1:2, at], taps[j, 2:3, at]) for j in range(3)]


def kernel(
    streams_hbm,
    taps_hbm,
    rates_hbm,
    residues_hbm,
    skip_hbm,
    out,
    streams,
    taps,
    rates,
    residues,
    skip,
    decay,
    sig,
    gate,
    base,
    inner,
    reach,
    edges_out,
    edges_in,
    gate_edges_out,
    gate_edges_in,
    sbuf,
    abuf,
    full,
    tbuf,
    bbuf,
    hbuf,
    cbuf,
    load_sem,
    piece_sem,
    halo_sem,
    a_send,
    a_recv,
    b_send,
    b_recv,
    c_send,
    c_recv,
):
    rows, width = sig.shape
    steps = rows // SUB
    modes = rates.shape[0]
    tiles = width // LANES
    piece = width // GROUP
    halves = piece // LANES
    me = lax.axis_index("ctx")
    count = lax.axis_size("ctx")
    outer = count // GROUP
    g = me // GROUP
    l = me - g * GROUP
    chip = l // 2
    core = l - chip * 2

    def member(k):
        pair = k // 2
        hop = 2 - pair + 3 * (pair // 2) - 2 * (pair // 3)
        return 2 * lax.rem(chip + hop, CHIPS) + lax.rem(core + 1 + k, 2)

    taps_load = pltpu.make_async_copy(taps_hbm, taps, load_sem.at[0])
    rates_load = pltpu.make_async_copy(rates_hbm, rates, load_sem.at[1])
    late_loads = [
        pltpu.make_async_copy(streams_hbm.at[0], streams.at[0], load_sem.at[2]),
        pltpu.make_async_copy(residues_hbm, residues, load_sem.at[3]),
        pltpu.make_async_copy(skip_hbm, skip, load_sem.at[4]),
    ]

    def piece_load(k):
        at = lanes(member(k), piece)
        return pltpu.make_async_copy(
            streams_hbm.at[pl.ds(1, 2), :, at], streams.at[pl.ds(1, 2), :, at], piece_sem.at[k]
        )

    taps_load.start()
    piece_load(0).start()
    rates_load.start()

    bar = pltpu.get_barrier_semaphore()

    def greet(ctx):
        pl.semaphore_signal(bar, inc=1, device_id={"ctx": ctx}, device_id_type=MESH)

    for k in range(1, outer):
        greet(lax.rem(g + k, outer) * GROUP + l)
    for k in range(1, GROUP):
        greet(g * GROUP + lax.rem(l + k, GROUP))
    greet(lax.rem(me + 1, count))
    greet(lax.rem(me + count - 1, count))

    for k in range(1, GROUP):
        piece_load(k).start()
    for load in late_loads:
        load.start()

    perm = gather_rows(rows)
    sub_row = lax.broadcasted_iota(jnp.int32, (SUB, LANES), 0)
    sub_pos = sub_row.astype(F32) * float(steps)
    to_end = sub_pos - float(steps * (SUB - 1))

    def signal_of(k):
        p = member(k)
        at = lanes(p, piece)
        piece_load(k).wait()
        one, one_edge = featurize(perm, streams, taps, 1, at)
        two, two_edge = featurize(perm, streams, taps, 2, at)
        row = lax.broadcasted_iota(jnp.int32, (rows, piece), 0)
        sig[:, at] = jnp.where((row == 0) | (row == SUB), 0.0, one * two)
        edge_row = lax.broadcasted_iota(jnp.int32, (SUB, piece), 0)
        edges = jnp.where(edge_row < 4, one_edge, two_edge)
        edges = jnp.concatenate(
            [edges[:, h * LANES : h * LANES + LANES] for h in range(halves)], axis=0
        ).astype(BF16)
        edges_out[p] = edges
        sbuf[p, halves * modes :, :] = edges

    def state_of(k):
        p = member(k)
        for half in range(halves):
            at = lanes(p * halves + half)
            factor = [
                jnp.broadcast_to(decay[pl.ds(m, 1), at], (SUB, LANES)) for m in range(modes)
            ]
            held = [sig[0:SUB, at]] * modes
            for b in range(1, steps):
                x = sig[SUB * b : SUB * b + SUB, at]
                held = [h * f + x for h, f in zip(held, factor)]
            ends = []
            for m in range(modes):
                weight = jnp.exp(to_end * rates[pl.ds(m, 1), at])
                ends.append(jnp.sum(held[m] * weight, axis=0, keepdims=True))
            sbuf[p, half * modes : half * modes + modes, :] = jnp.concatenate(
                ends, axis=0
            ).astype(BF16)

    def first_send(k):
        to = member(k)
        return pltpu.make_async_remote_copy(
            src_ref=sbuf.at[to],
            dst_ref=abuf.at[l],
            send_sem=a_send,
            recv_sem=a_recv,
            device_id={"ctx": g * GROUP + to},
            device_id_type=MESH,
        )

    def halo_send(source, target, which):
        return pltpu.make_async_remote_copy(
            src_ref=source,
            dst_ref=target,
            send_sem=halo_sem.at[2 * which],
            recv_sem=halo_sem.at[2 * which + 1],
            device_id={"ctx": lax.rem(me + 1, count)},
            device_id_type=MESH,
        )

    taps_load.wait()
    signal_of(0)
    rates_load.wait()
    decay[...] = jnp.exp(-rates[...])

    def early_step(k, carry):
        state_of(k)
        signal_of(k + 1)
        return carry

    lax.fori_loop(0, GROUP - 2, early_step, 0)
    pl.semaphore_wait(bar, GROUP - 1 + outer - 1 + 2)

    def first_send_step(k, carry):
        first_send(k).start()
        return carry

    lax.fori_loop(0, GROUP - 2, first_send_step, 0)
    state_of(GROUP - 2)
    first_send(GROUP - 2).start()
    signal_of(GROUP - 1)
    halo = halo_send(edges_out, edges_in, 0)

    @pl.when(me < count - 1)
    def _():
        halo.start()

    state_of(GROUP - 1)
    abuf[l] = sbuf[l]

    for load in late_loads:
        load.wait()

    def gate_step(p, carry):
        at = lanes(p, piece)
        features, edges = featurize(perm, streams, taps, 0, at)
        gate[:, at] = features
        gate_edges_out[p] = jnp.concatenate(
            [edges[:, h * LANES : h * LANES + LANES] for h in range(halves)], axis=0
        ).astype(BF16)
        return carry

    lax.fori_loop(0, GROUP, gate_step, 0)
    gate_halo = halo_send(gate_edges_out, gate_edges_in, 1)

    @pl.when(me < count - 1)
    def _():
        gate_halo.start()

    def reach_step(c, carry):
        at = lanes(c)
        for m in range(modes):
            rate = rates[pl.ds(m, 1), at]
            lead = residues[pl.ds(m, 1), at] * decay[pl.ds(m, 1), at]
            reach[c, m] = lead * jnp.exp(-sub_pos * rate)
        return carry

    lax.fori_loop(0, tiles, reach_step, 0)

    for k in range(1, outer):

        @pl.when(k > g)
        def _():
            bbuf[k - 1] = jnp.zeros(bbuf.shape[1:], BF16)

    mine = [lanes(l * halves + half) for half in range(halves)]
    my_rates = [rates[:, at] for at in mine]
    my_weights = [edge_weights(taps, at) for at in mine]

    def power(n):
        return [jnp.exp(rate * (-float(n))) for rate in my_rates]

    def unpack(message):
        value = message.astype(F32)
        body = [value[h * modes : h * modes + modes] for h in range(halves)]
        edge = value[halves * modes :]
        return body, [edge[h * SUB : h * SUB + SUB] for h in range(halves)]

    def with_edge(body, first, second, own, before):
        done = []
        for h in range(halves):
            s = edge_signal(my_weights[h], own[h], before[h])
            done.append(body[h] + first[h] * s[0:1] + second[h] * s[1:2])
        return done

    chunk_decay = power(rows)
    to_first = power(rows - 1)
    to_second = power(rows - 2)
    others = pl.ds(0, GROUP - 1)
    pltpu.make_async_copy(sbuf.at[others], abuf.at[others], a_recv).wait()
    total, first_edge = unpack(abuf[0])
    first_body = total
    before = first_edge
    for k in range(1, GROUP):
        body, edge = unpack(abuf[k])
        body = with_edge(body, to_first, to_second, edge, before)
        for h in range(halves):
            full[k, h * modes : h * modes + modes, :] = body[h]
        total = [t * d + b for t, d, b in zip(total, chunk_decay, body)]
        before = edge
    group_edge = [jnp.where((sub_row & 3) < 2, a, b) for a, b in zip(first_edge, before)]
    tbuf[...] = jnp.concatenate(total + group_edge, axis=0).astype(BF16)

    def group_copy(k):
        return pltpu.make_async_remote_copy(
            src_ref=tbuf,
            dst_ref=bbuf.at[k - 1],
            send_sem=b_send.at[k - 1],
            recv_sem=b_recv.at[k - 1],
            device_id={"ctx": lax.rem(g + k, outer) * GROUP + l},
            device_id_type=MESH,
        )

    for k in (4, 5, 3, 6, 2, 7, 1):

        @pl.when(g + k < outer)
        def _():
            group_copy(k).start()

    @pl.when(me > 0)
    def _():
        halo.wait_recv()

    @pl.when(me == 0)
    def _():
        edges_in[...] = jnp.zeros_like(edges_in)

    def edge_step(p, carry):
        for h in range(halves):
            at = lanes(p * halves + h)
            part = slice(h * SUB, h * SUB + SUB)
            s = edge_signal(
                edge_weights(taps, at),
                edges_out[p].astype(F32)[part],
                edges_in[p].astype(F32)[part],
            )
            sig[0:1, at] = s[0:1]
            sig[SUB : SUB + 1, at] = s[1:2]
        return carry

    lax.fori_loop(0, GROUP, edge_step, 0)

    def own_step(c, carry):
        at = lanes(c)
        factor = [jnp.broadcast_to(decay[pl.ds(m, 1), at], (SUB, LANES)) for m in range(modes)]
        weight = [jnp.broadcast_to(residues[pl.ds(m, 1), at], (SUB, LANES)) for m in range(modes)]
        direct = jnp.broadcast_to(skip[0:1, at], (SUB, LANES))
        held = None
        for b in range(steps):
            x = sig[SUB * b : SUB * b + SUB, at]
            held = [x] * modes if b == 0 else [h * f + x for h, f in zip(held, factor)]
            terms = direct * x
            for h, w in zip(held, weight):
                terms = terms + h * w
            base[SUB * b : SUB * b + SUB, at] = terms
        for m in range(modes):
            rate = rates[pl.ds(m, 1), at]
            begin = jnp.where(sub_row < 1, 0.0, pltpu.roll(held[m], 1, 0))
            for back_rows in (1, 2, 4):
                begin = begin + jnp.exp(rate * (-float(steps * back_rows))) * jnp.where(
                    sub_row < back_rows, 0.0, pltpu.roll(begin, back_rows, 0)
                )
            inner[c, m] = weight[m] * factor[m] * begin
        return carry

    lax.fori_loop(0, tiles, own_step, 0)

    @pl.when(me > 0)
    def _():
        gate_halo.wait_recv()

    @pl.when(me == 0)
    def _():
        gate_edges_in[...] = jnp.zeros_like(gate_edges_in)

    def gate_edge_step(p, carry):
        for h in range(halves):
            at = lanes(p * halves + h)
            part = slice(h * SUB, h * SUB + SUB)
            f = edge_features(
                [taps[j, 0:1, at] for j in range(3)],
                gate_edges_out[p].astype(F32)[part],
                gate_edges_in[p].astype(F32)[part],
            )
            gate[0:1, at] = f[0:1]
            gate[SUB : SUB + 1, at] = f[1:2]
        return carry

    lax.fori_loop(0, GROUP, gate_edge_step, 0)

    group_decay = power(rows * GROUP)
    group_first = power(rows * GROUP - 1)
    group_second = power(rows * GROUP - 2)
    for k in range(1, outer):

        @pl.when(k <= g)
        def _():
            pltpu.make_async_copy(tbuf, bbuf.at[k - 1], b_recv.at[k - 1]).wait()

    held = [jnp.zeros((modes, LANES), F32)] * halves
    before = [jnp.zeros((SUB, LANES), F32)] * halves
    for k in range(outer - 1, 0, -1):
        body, edge = unpack(bbuf[k - 1])
        body = with_edge(body, group_first, group_second, edge, before)
        held = [h * d + b for h, d, b in zip(held, group_decay, body)]
        before = edge
    for k in range(GROUP):
        if k == 1:
            body = with_edge(first_body, to_first, to_second, first_edge, before)
        elif k > 1:
            body = [full[k - 1, h * modes : h * modes + modes, :] for h in range(halves)]
        if k > 0:
            held = [h * d + b for h, d, b in zip(held, chunk_decay, body)]
        hbuf[k] = jnp.concatenate(held, axis=0).astype(BF16)

    def last_send(k):
        to = member(k)
        return pltpu.make_async_remote_copy(
            src_ref=hbuf.at[to],
            dst_ref=cbuf.at[l],
            send_sem=c_send,
            recv_sem=c_recv.at[l],
            device_id={"ctx": g * GROUP + to},
            device_id_type=MESH,
        )

    def last_send_step(k, carry):
        last_send(k).start()
        return carry

    lax.fori_loop(0, GROUP - 1, last_send_step, 0)
    cbuf[l] = hbuf[l]
    back = scatter_rows(rows)

    def mix_of(p):
        mixed = []
        entering = cbuf[p].astype(F32)
        for half in range(halves):
            c = p * halves + half
            at = lanes(c)
            factor = [
                jnp.broadcast_to(decay[pl.ds(m, 1), at], (SUB, LANES)) for m in range(modes)
            ]
            term = [
                inner[c, m] + reach[c, m] * entering[half * modes + m : half * modes + m + 1]
                for m in range(modes)
            ]
            column = []
            for b in range(steps):
                terms = base[SUB * b : SUB * b + SUB, at]
                for h in term:
                    terms = terms + h
                column.append(gate[SUB * b : SUB * b + SUB, at] * terms)
                if b < steps - 1:
                    term = [h * f for h, f in zip(term, factor)]
            mixed.append(jnp.concatenate(column, axis=0).astype(BF16))
        mixed = jnp.concatenate(mixed, axis=1)
        out[:, lanes(p, piece)] = jnp.dot(back, mixed, preferred_element_type=F32).astype(BF16)

    mix_of(l)

    def mix_step(k, carry):
        p = member(GROUP - 2 - k)
        pltpu.make_async_copy(hbuf.at[p], cbuf.at[p], c_recv.at[p]).wait()
        mix_of(p)
        return carry

    lax.fori_loop(0, GROUP - 1, mix_step, 0)

    @pl.when(me < count - 1)
    def _():
        halo.wait_send()
        gate_halo.wait_send()

    pltpu.make_async_copy(sbuf.at[others], abuf.at[others], a_send).wait()
    pltpu.make_async_copy(hbuf.at[others], cbuf.at[others], c_send).wait()
    for k in range(1, outer):

        @pl.when(g + k < outer)
        def _():
            group_copy(k).wait_send()


def local(streams, short_filter, rates, residues, skip):
    _, rows, width = streams.shape
    modes = rates.shape[0]
    tiles = width // LANES
    halves = tiles // GROUP
    outer = lax.axis_size("ctx") // GROUP
    args = (streams, short_filter, rates, residues, skip[None, :])
    wide = pltpu.VMEM((rows, width), F32)
    per_mode = pltpu.VMEM((tiles, modes, SUB, LANES), F32)
    edges = pltpu.VMEM((GROUP, halves * SUB, LANES), BF16)
    body = halves * modes
    message = body + halves * SUB
    dma = pltpu.SemaphoreType.DMA
    return pl.pallas_call(
        kernel,
        out_shape=pltpu.VMEM((rows, width), BF16),
        in_specs=[pl.BlockSpec(memory_space=pltpu.HBM)] * len(args),
        out_specs=pl.BlockSpec(memory_space=pltpu.VMEM),
        scratch_shapes=[
            pltpu.VMEM(streams.shape, BF16),
            pltpu.VMEM(short_filter.shape, F32),
            pltpu.VMEM(rates.shape, F32),
            pltpu.VMEM(rates.shape, F32),
            pltpu.VMEM((1, width), F32),
            pltpu.VMEM(rates.shape, F32),
            wide,
            wide,
            wide,
            per_mode,
            per_mode,
            edges,
            edges,
            edges,
            edges,
            pltpu.VMEM((GROUP, message, LANES), BF16),
            pltpu.VMEM((GROUP, message, LANES), BF16),
            pltpu.VMEM((GROUP, body, LANES), F32),
            pltpu.VMEM((message, LANES), BF16),
            pltpu.VMEM((outer - 1, message, LANES), BF16),
            pltpu.VMEM((GROUP, body, LANES), BF16),
            pltpu.VMEM((GROUP, body, LANES), BF16),
            dma((5,)),
            dma((GROUP,)),
            dma((4,)),
            dma,
            dma,
            dma((outer - 1,)),
            dma((outer - 1,)),
            dma,
            dma((GROUP,)),
        ],
        compiler_params=pltpu.CompilerParams(
            collective_id=0, has_side_effects=True, vmem_limit_bytes=24 * 1024 * 1024
        ),
        name="mixer",
    )(*(pltpu.with_memory_space_constraint(a, pltpu.HBM) for a in args))


def solution(mesh):
    placed = (
        P(None, "ctx", "chan"),
        P(None, None, "chan"),
        P(None, "chan"),
        P(None, "chan"),
        P("chan"),
    )
    return jax.shard_map(
        local, mesh=mesh, in_specs=placed, out_specs=P("ctx", "chan"), check_vma=False
    )
```

time: 31 us -> 22.5 us (0.73)
  the two profiles are of different devices: /device:TPU:209 before, /device:TPU:1 now
where the time goes in v1:
time: 22.5 us
  Pallas kernels  21.7 us (96%)
  local copies, waits for them, and re-layouts  0.8 us (4%)
    pallas_call x1, Pallas kernels, local(): pl.pallas_call(kernel, out_shape=pltpu.VMEM((rows, width), BF16), in_spec...  21.7 us
    unnamed x1, local copies, waits for them, and re-layouts  0.8 us

profile of v1, /device:TPU:1, one launch (start us, length us, event | category | flops | bytes accessed | tf_op | source)
XLA Modules:
  0.0 22.5 jit_solution(707571091522543317)
XLA Ops:
  0.0 21.7 %mixer.1 = bf16[128,2048]{1,0:T(8,128)(2,1)S(1)} custom-call(bf16[3,128,2048]{2,1,0:T(8,128)(2,1)} %streams_hbm.1, f32[3,3,2048]{2,1,0:T(4,128)} %taps_hbm.1, f32[16,2048]{1,0:T(8,128)} %rates_hbm.1, f32[16,2048]{1,0:T(8,128)} %residues_hbm.1, f32[1,2048]{1,0:T(1,128)} %bitcast.1), custom_call_target="tpu_custom_call" | custom-call | tf_op jit(solution)/shard_map/mixer/pallas_call | solution.py:514
  21.7 0.8 %copy.7 = bf16[128,2048]{1,0:T(8,128)(2,1)} copy(bf16[128,2048]{1,0:T(8,128)(2,1)S(1)} %mixer.1) | data formatting | bytes 1048576

commit v2 on v1

--- a/solution.py
+++ b/solution.py
@@ -7,6 +7,8 @@
 
 MESH = pl.DeviceIdType.MESH
 LANES = 128
+ANSWER_AT = 1
+LATE_TILES = 4
 SUB = 8
 GROUP = 8
 CHIPS = GROUP // 2
@@ -86,13 +88,20 @@
     sbuf,
     abuf,
     full,
+    extra,
     tbuf,
     bbuf,
     hbuf,
     cbuf,
+    entering,
+    ready_a,
+    ready_b,
     load_sem,
     piece_sem,
     halo_sem,
+    mates_in,
+    groups_in,
+    next_in,
     a_send,
     a_recv,
     b_send,
@@ -109,10 +118,15 @@
     me = lax.axis_index("ctx")
     count = lax.axis_size("ctx")
     outer = count // GROUP
+    half = outer // 2
     g = me // GROUP
     l = me - g * GROUP
     chip = l // 2
     core = l - chip * 2
+
+    def earlier_mates(at):
+        c = at // 2
+        return 2 * (c + c // 2 - 2 * (c // 3)) + 1 - (at - 2 * c)
 
     def member(k):
         pair = k // 2
@@ -142,12 +156,33 @@
     def greet(ctx):
         pl.semaphore_signal(bar, inc=1, device_id={"ctx": ctx}, device_id_type=MESH)
 
+    def along(other):
+        return other * GROUP + l
+
+    for k in range(1, GROUP):
+        mate = lax.rem(l + k, GROUP)
+
+        @pl.when(earlier_mates(mate) > earlier_mates(l))
+        def _():
+            greet(g * GROUP + mate)
+
+    first_half = g < half
     for k in range(1, outer):
-        greet(lax.rem(g + k, outer) * GROUP + l)
-    for k in range(1, GROUP):
-        greet(g * GROUP + lax.rem(l + k, GROUP))
-    greet(lax.rem(me + 1, count))
-    greet(lax.rem(me + count - 1, count))
+
+        @pl.when((g + k < outer) & (first_half | (k == 1)))
+        def _():
+            greet(along(g + k))
+
+    @pl.when(g > half)
+    def _():
+        greet(along(g - 1))
+
+    greetings = (
+        earlier_mates(l)
+        + jnp.minimum(g, half)
+        + jnp.where(g > half, 1, 0)
+        + jnp.where((g >= half) & (g < outer - 1), 1, 0)
+    )
 
     for k in range(1, GROUP):
         piece_load(k).start()
@@ -225,8 +260,43 @@
         signal_of(k + 1)
         return carry
 
-    lax.fori_loop(0, GROUP - 2, early_step, 0)
-    pl.semaphore_wait(bar, GROUP - 1 + outer - 1 + 2)
+    lax.fori_loop(0, ANSWER_AT, early_step, 0)
+
+    @pl.when(greetings > 0)
+    def _():
+        pl.semaphore_wait(bar, greetings)
+
+    for k in range(1, GROUP):
+        mate = lax.rem(l + k, GROUP)
+
+        @pl.when(earlier_mates(mate) < earlier_mates(l))
+        def _():
+            pl.semaphore_signal(
+                mates_in, inc=1, device_id={"ctx": g * GROUP + mate}, device_id_type=MESH
+            )
+
+    def tell_group(other, k):
+        pl.semaphore_signal(
+            groups_in.at[k - 1], inc=1, device_id={"ctx": along(other)}, device_id_type=MESH
+        )
+
+    for k in range(1, outer):
+
+        @pl.when((k <= g) & (g - k < half))
+        def _():
+            tell_group(g - k, k)
+
+    @pl.when((g > half) & (g < outer - 1))
+    def _():
+        tell_group(g - 1, 2)
+
+    lax.fori_loop(ANSWER_AT, GROUP - 2, early_step, 0)
+    answers = GROUP - 1 - earlier_mates(l)
+
+    @pl.when(answers > 0)
+    def _():
+        pl.semaphore_wait(mates_in, answers)
+
 
     def first_send_step(k, carry):
         first_send(k).start()
@@ -236,14 +306,14 @@
     state_of(GROUP - 2)
     first_send(GROUP - 2).start()
     signal_of(GROUP - 1)
-    halo = halo_send(edges_out, edges_in, 0)
-
-    @pl.when(me < count - 1)
-    def _():
-        halo.start()
-
     state_of(GROUP - 1)
     abuf[l] = sbuf[l]
+
+    @pl.when(g == half + 1)
+    def _():
+        pl.semaphore_wait(groups_in.at[1], 1)
+        tell_group(half, 3)
+
 
     for load in late_loads:
         load.wait()
@@ -258,11 +328,23 @@
         return carry
 
     lax.fori_loop(0, GROUP, gate_step, 0)
+    halo = halo_send(edges_out, edges_in, 0)
     gate_halo = halo_send(gate_edges_out, gate_edges_in, 1)
 
-    @pl.when(me < count - 1)
-    def _():
+    @pl.when(l < GROUP - 1)
+    def _():
+        halo.start()
         gate_halo.start()
+
+    @pl.when((l == 0) & (g < outer - 1))
+    def _():
+        @pl.when(first_half)
+        def _():
+            pl.semaphore_wait(groups_in.at[0], 1)
+
+        pl.semaphore_signal(
+            next_in, inc=1, device_id={"ctx": me + GROUP - 1}, device_id_type=MESH
+        )
 
     def reach_step(c, carry):
         at = lanes(c)
@@ -273,89 +355,6 @@
         return carry
 
     lax.fori_loop(0, tiles, reach_step, 0)
-
-    for k in range(1, outer):
-
-        @pl.when(k > g)
-        def _():
-            bbuf[k - 1] = jnp.zeros(bbuf.shape[1:], BF16)
-
-    mine = [lanes(l * halves + half) for half in range(halves)]
-    my_rates = [rates[:, at] for at in mine]
-    my_weights = [edge_weights(taps, at) for at in mine]
-
-    def power(n):
-        return [jnp.exp(rate * (-float(n))) for rate in my_rates]
-
-    def unpack(message):
-        value = message.astype(F32)
-        body = [value[h * modes : h * modes + modes] for h in range(halves)]
-        edge = value[halves * modes :]
-        return body, [edge[h * SUB : h * SUB + SUB] for h in range(halves)]
-
-    def with_edge(body, first, second, own, before):
-        done = []
-        for h in range(halves):
-            s = edge_signal(my_weights[h], own[h], before[h])
-            done.append(body[h] + first[h] * s[0:1] + second[h] * s[1:2])
-        return done
-
-    chunk_decay = power(rows)
-    to_first = power(rows - 1)
-    to_second = power(rows - 2)
-    others = pl.ds(0, GROUP - 1)
-    pltpu.make_async_copy(sbuf.at[others], abuf.at[others], a_recv).wait()
-    total, first_edge = unpack(abuf[0])
-    first_body = total
-    before = first_edge
-    for k in range(1, GROUP):
-        body, edge = unpack(abuf[k])
-        body = with_edge(body, to_first, to_second, edge, before)
-        for h in range(halves):
-            full[k, h * modes : h * modes + modes, :] = body[h]
-        total = [t * d + b for t, d, b in zip(total, chunk_decay, body)]
-        before = edge
-    group_edge = [jnp.where((sub_row & 3) < 2, a, b) for a, b in zip(first_edge, before)]
-    tbuf[...] = jnp.concatenate(total + group_edge, axis=0).astype(BF16)
-
-    def group_copy(k):
-        return pltpu.make_async_remote_copy(
-            src_ref=tbuf,
-            dst_ref=bbuf.at[k - 1],
-            send_sem=b_send.at[k - 1],
-            recv_sem=b_recv.at[k - 1],
-            device_id={"ctx": lax.rem(g + k, outer) * GROUP + l},
-            device_id_type=MESH,
-        )
-
-    for k in (4, 5, 3, 6, 2, 7, 1):
-
-        @pl.when(g + k < outer)
-        def _():
-            group_copy(k).start()
-
-    @pl.when(me > 0)
-    def _():
-        halo.wait_recv()
-
-    @pl.when(me == 0)
-    def _():
-        edges_in[...] = jnp.zeros_like(edges_in)
-
-    def edge_step(p, carry):
-        for h in range(halves):
-            at = lanes(p * halves + h)
-            part = slice(h * SUB, h * SUB + SUB)
-            s = edge_signal(
-                edge_weights(taps, at),
-                edges_out[p].astype(F32)[part],
-                edges_in[p].astype(F32)[part],
-            )
-            sig[0:1, at] = s[0:1]
-            sig[SUB : SUB + 1, at] = s[1:2]
-        return carry
-
-    lax.fori_loop(0, GROUP, edge_step, 0)
 
     def own_step(c, carry):
         at = lanes(c)
@@ -380,7 +379,168 @@
             inner[c, m] = weight[m] * factor[m] * begin
         return carry
 
-    lax.fori_loop(0, tiles, own_step, 0)
+    early_tiles = tiles - LATE_TILES * (earlier_mates(l) // 2)
+    lax.fori_loop(0, early_tiles, own_step, 0)
+
+    @pl.when((l == GROUP - 1) & (g < outer - 1))
+    def _():
+        pl.semaphore_wait(next_in, 1)
+        halo.start()
+        gate_halo.start()
+
+    for k in range(1, outer):
+
+        @pl.when(k > g)
+        def _():
+            bbuf[k - 1] = jnp.zeros(bbuf.shape[1:], BF16)
+
+    mine = [lanes(l * halves + half) for half in range(halves)]
+    my_rates = [rates[:, at] for at in mine]
+    my_weights = [edge_weights(taps, at) for at in mine]
+
+    def power(n):
+        return [jnp.exp(rate * (-float(n))) for rate in my_rates]
+
+    def unpack(message):
+        value = message.astype(F32)
+        body = [value[h * modes : h * modes + modes] for h in range(halves)]
+        edge = value[halves * modes :]
+        return body, [edge[h * SUB : h * SUB + SUB] for h in range(halves)]
+
+    def with_edge(body, first, second, own, before):
+        done = []
+        for h in range(halves):
+            s = edge_signal(my_weights[h], own[h], before[h])
+            done.append(body[h] + first[h] * s[0:1] + second[h] * s[1:2])
+        return done
+
+    chunk_decay = power(rows)
+    to_first = power(rows - 1)
+    to_second = power(rows - 2)
+    others = pl.ds(0, GROUP - 1)
+    pltpu.make_async_copy(sbuf.at[others], abuf.at[others], a_recv).wait()
+    total, first_edge = unpack(abuf[0])
+    first_body = total
+    before = first_edge
+    for k in range(1, GROUP):
+        body, edge = unpack(abuf[k])
+        body = with_edge(body, to_first, to_second, edge, before)
+        for h in range(halves):
+            full[k, h * modes : h * modes + modes, :] = body[h]
+        total = [t * d + b for t, d, b in zip(total, chunk_decay, body)]
+        before = edge
+    group_edge = [jnp.where((sub_row & 3) < 2, a, b) for a, b in zip(first_edge, before)]
+    tbuf[...] = jnp.concatenate(total + group_edge, axis=0).astype(BF16)
+
+    def group_copy(k):
+        return pltpu.make_async_remote_copy(
+            src_ref=tbuf,
+            dst_ref=bbuf.at[k - 1],
+            send_sem=b_send.at[k - 1],
+            recv_sem=b_recv.at[k - 1],
+            device_id={"ctx": along(g + k)},
+            device_id_type=MESH,
+        )
+
+    def group_send(k):
+        @pl.when(g + k < outer)
+        def _():
+            waited = ((k == 1) & (l == 0)) | ((k == 2) & (g == half + 1))
+
+            @pl.when((first_half | (k > 1)) & jnp.logical_not(waited))
+            def _():
+                pl.semaphore_wait(groups_in.at[k - 1], 1)
+
+            group_copy(k).start()
+
+    for k in range(1, outer):
+        group_send(k)
+
+    one_up = power(-1)
+    two_up = power(-2)
+
+    def boost(own, before):
+        done = []
+        for h in range(halves):
+            s = edge_signal(my_weights[h], own[h], before[h])
+            done.append(one_up[h] * s[0:1] + two_up[h] * s[1:2])
+        return done
+
+    before = first_edge
+    for k in range(1, GROUP):
+        edge = unpack(abuf[k])[1]
+        extra[k] = jnp.concatenate(boost(edge, before), axis=0)
+        before = edge
+
+    group_decay = power(rows * GROUP)
+    group_first = power(rows * GROUP - 1)
+    group_second = power(rows * GROUP - 2)
+    for k in range(1, outer):
+
+        @pl.when(k <= g)
+        def _():
+            pltpu.make_async_copy(tbuf, bbuf.at[k - 1], b_recv.at[k - 1]).wait()
+
+    held = [jnp.zeros((modes, LANES), F32)] * halves
+    before = [jnp.zeros((SUB, LANES), F32)] * halves
+    for k in range(outer - 1, 0, -1):
+        body, edge = unpack(bbuf[k - 1])
+        body = with_edge(body, group_first, group_second, edge, before)
+        held = [h * d + b for h, d, b in zip(held, group_decay, body)]
+        before = edge
+    extra[0] = jnp.concatenate(boost(first_edge, before), axis=0)
+    for k in range(GROUP):
+        if k == 1:
+            body = with_edge(first_body, to_first, to_second, first_edge, before)
+        elif k > 1:
+            body = [full[k - 1, h * modes : h * modes + modes, :] for h in range(halves)]
+        if k > 0:
+            held = [h * d + b for h, d, b in zip(held, chunk_decay, body)]
+        hbuf[k] = (jnp.concatenate(held, axis=0) + extra[k]).astype(BF16)
+
+    def last_send(k):
+        to = member(k)
+        return pltpu.make_async_remote_copy(
+            src_ref=hbuf.at[to],
+            dst_ref=cbuf.at[l],
+            send_sem=c_send,
+            recv_sem=c_recv.at[l],
+            device_id={"ctx": g * GROUP + to},
+            device_id_type=MESH,
+        )
+
+    def last_send_step(k, carry):
+        last_send(k).start()
+        return carry
+
+    lax.fori_loop(0, GROUP - 1, last_send_step, 0)
+    cbuf[l] = hbuf[l]
+    back = scatter_rows(rows)
+    lax.fori_loop(early_tiles, tiles, own_step, 0)
+
+    @pl.when(me > 0)
+    def _():
+        halo.wait_recv()
+
+    @pl.when(me == 0)
+    def _():
+        edges_in[...] = jnp.zeros_like(edges_in)
+
+    def edge_step(p, carry):
+        for h in range(halves):
+            at = lanes(p * halves + h)
+            part = slice(h * SUB, h * SUB + SUB)
+            s = edge_signal(
+                edge_weights(taps, at),
+                edges_out[p].astype(F32)[part],
+                edges_in[p].astype(F32)[part],
+            )
+            ahead = jnp.sum(residues[:, at] * jnp.exp(rates[:, at]), axis=0, keepdims=True)
+            base[0:1, at] += skip[0:1, at] * s[0:1] - ahead * s[1:2]
+            base[SUB : SUB + 1, at] += skip[0:1, at] * s[1:2]
+        return carry
+
+    lax.fori_loop(0, GROUP, edge_step, 0)
 
     @pl.when(me > 0)
     def _():
@@ -405,53 +565,9 @@
 
     lax.fori_loop(0, GROUP, gate_edge_step, 0)
 
-    group_decay = power(rows * GROUP)
-    group_first = power(rows * GROUP - 1)
-    group_second = power(rows * GROUP - 2)
-    for k in range(1, outer):
-
-        @pl.when(k <= g)
-        def _():
-            pltpu.make_async_copy(tbuf, bbuf.at[k - 1], b_recv.at[k - 1]).wait()
-
-    held = [jnp.zeros((modes, LANES), F32)] * halves
-    before = [jnp.zeros((SUB, LANES), F32)] * halves
-    for k in range(outer - 1, 0, -1):
-        body, edge = unpack(bbuf[k - 1])
-        body = with_edge(body, group_first, group_second, edge, before)
-        held = [h * d + b for h, d, b in zip(held, group_decay, body)]
-        before = edge
-    for k in range(GROUP):
-        if k == 1:
-            body = with_edge(first_body, to_first, to_second, first_edge, before)
-        elif k > 1:
-            body = [full[k - 1, h * modes : h * modes + modes, :] for h in range(halves)]
-        if k > 0:
-            held = [h * d + b for h, d, b in zip(held, chunk_decay, body)]
-        hbuf[k] = jnp.concatenate(held, axis=0).astype(BF16)
-
-    def last_send(k):
-        to = member(k)
-        return pltpu.make_async_remote_copy(
-            src_ref=hbuf.at[to],
-            dst_ref=cbuf.at[l],
-            send_sem=c_send,
-            recv_sem=c_recv.at[l],
-            device_id={"ctx": g * GROUP + to},
-            device_id_type=MESH,
-        )
-
-    def last_send_step(k, carry):
-        last_send(k).start()
-        return carry
-
-    lax.fori_loop(0, GROUP - 1, last_send_step, 0)
-    cbuf[l] = hbuf[l]
-    back = scatter_rows(rows)
-
-    def mix_of(p):
-        mixed = []
-        entering = cbuf[p].astype(F32)
+
+    def mix_of(p, ready):
+        entering[...] = cbuf[p].astype(F32)
         for half in range(halves):
             c = p * halves + half
             at = lanes(c)
@@ -459,7 +575,7 @@
                 jnp.broadcast_to(decay[pl.ds(m, 1), at], (SUB, LANES)) for m in range(modes)
             ]
             term = [
-                inner[c, m] + reach[c, m] * entering[half * modes + m : half * modes + m + 1]
+                inner[c, m] + reach[c, m] * entering[pl.ds(half * modes + m, 1), :]
                 for m in range(modes)
             ]
             column = []
@@ -470,19 +586,31 @@
                 column.append(gate[SUB * b : SUB * b + SUB, at] * terms)
                 if b < steps - 1:
                     term = [h * f for h, f in zip(term, factor)]
-            mixed.append(jnp.concatenate(column, axis=0).astype(BF16))
-        mixed = jnp.concatenate(mixed, axis=1)
-        out[:, lanes(p, piece)] = jnp.dot(back, mixed, preferred_element_type=F32).astype(BF16)
-
-    mix_of(l)
-
-    def mix_step(k, carry):
-        p = member(GROUP - 2 - k)
+            ready[:, half * LANES : half * LANES + LANES] = jnp.concatenate(
+                column, axis=0
+            ).astype(BF16)
+
+    def put_back(p, ready):
+        out[:, lanes(p, piece)] = jnp.dot(
+            back, ready[...], preferred_element_type=F32
+        ).astype(BF16)
+
+    def mix_next(k, ready, last_ready):
+        p = member(k)
         pltpu.make_async_copy(hbuf.at[p], cbuf.at[p], c_recv.at[p]).wait()
-        mix_of(p)
-        return carry
-
-    lax.fori_loop(0, GROUP - 1, mix_step, 0)
+        put_back(member(k + 1), last_ready)
+        mix_of(p, ready)
+
+    mix_of(l, ready_a)
+
+    def mix_pair(j, carry):
+        mix_next(GROUP - 2 - 2 * j, ready_b, ready_a)
+        mix_next(GROUP - 3 - 2 * j, ready_a, ready_b)
+        return carry
+
+    lax.fori_loop(0, GROUP // 2 - 1, mix_pair, 0)
+    mix_next(0, ready_b, ready_a)
+    put_back(member(0), ready_b)
 
     @pl.when(me < count - 1)
     def _():
@@ -535,13 +663,20 @@
             pltpu.VMEM((GROUP, message, LANES), BF16),
             pltpu.VMEM((GROUP, message, LANES), BF16),
             pltpu.VMEM((GROUP, body, LANES), F32),
+            pltpu.VMEM((GROUP, body, LANES), F32),
             pltpu.VMEM((message, LANES), BF16),
             pltpu.VMEM((outer - 1, message, LANES), BF16),
             pltpu.VMEM((GROUP, body, LANES), BF16),
             pltpu.VMEM((GROUP, body, LANES), BF16),
+            pltpu.VMEM((body, LANES), F32),
+            pltpu.VMEM((rows, halves * LANES), BF16),
+            pltpu.VMEM((rows, halves * LANES), BF16),
             dma((5,)),
             dma((GROUP,)),
             dma((4,)),
+            pltpu.SemaphoreType.REGULAR,
+            pltpu.SemaphoreType.REGULAR((outer - 1,)),
+            pltpu.SemaphoreType.REGULAR,
             dma,
             dma,
             dma((outer - 1,)),

time: 22.5 us -> 20.6 us (0.916)
  the two profiles are of different devices: /device:TPU:1 before, /device:TPU:240 now
where the time goes in v2:
time: 20.6 us; the launch traced here: 20.5 us
  Pallas kernels  19.7 us (96%)
  local copies, waits for them, and re-layouts  0.8 us (4%)
    pallas_call x1, Pallas kernels, local(): pl.pallas_call(kernel, out_shape=pltpu.VMEM((rows, width), BF16), in_spec...  19.7 us
    unnamed x1, local copies, waits for them, and re-layouts  0.8 us

profile of v2, /device:TPU:240, one launch (start us, length us, event | category | flops | bytes accessed | tf_op | source)
XLA Modules:
  0.0 20.5 jit_solution(11613791636675375630)
XLA Ops:
  0.0 19.7 %mixer.1 = bf16[128,2048]{1,0:T(8,128)(2,1)S(1)} custom-call(bf16[3,128,2048]{2,1,0:T(8,128)(2,1)} %streams_hbm.1, f32[3,3,2048]{2,1,0:T(4,128)} %taps_hbm.1, f32[16,2048]{1,0:T(8,128)} %rates_hbm.1, f32[16,2048]{1,0:T(8,128)} %residues_hbm.1, f32[1,2048]{1,0:T(1,128)} %bitcast.1), custom_call_target="tpu_custom_call" | custom-call | tf_op jit(solution)/shard_map/mixer/pallas_call | solution.py:642
  19.7 0.8 %copy.7 = bf16[128,2048]{1,0:T(8,128)(2,1)} copy(bf16[128,2048]{1,0:T(8,128)(2,1)S(1)} %mixer.1) | data formatting | bytes 1048576

commit v3 on v2

--- a/solution.py
+++ b/solution.py
@@ -7,8 +7,12 @@
 
 MESH = pl.DeviceIdType.MESH
 LANES = 128
-ANSWER_AT = 1
-LATE_TILES = 4
+LAST_ANSWER_AT = 6
+ANSWER_LESS = 2
+EARLY_TILES = 10
+EARLY_LESS = 3
+MIDDLE_TILES = 4
+FEW_MIDDLE = 0
 SUB = 8
 GROUP = 8
 CHIPS = GROUP // 2
@@ -99,7 +103,6 @@
     load_sem,
     piece_sem,
     halo_sem,
-    mates_in,
     groups_in,
     next_in,
     a_send,
@@ -124,9 +127,7 @@
     chip = l // 2
     core = l - chip * 2
 
-    def earlier_mates(at):
-        c = at // 2
-        return 2 * (c + c // 2 - 2 * (c // 3)) + 1 - (at - 2 * c)
+    order = chip + chip // 2 - 2 * (chip // 3)
 
     def member(k):
         pair = k // 2
@@ -160,11 +161,7 @@
         return other * GROUP + l
 
     for k in range(1, GROUP):
-        mate = lax.rem(l + k, GROUP)
-
-        @pl.when(earlier_mates(mate) > earlier_mates(l))
-        def _():
-            greet(g * GROUP + mate)
+        greet(g * GROUP + lax.rem(l + k, GROUP))
 
     first_half = g < half
     for k in range(1, outer):
@@ -178,7 +175,8 @@
         greet(along(g - 1))
 
     greetings = (
-        earlier_mates(l)
+        GROUP
+        - 1
         + jnp.minimum(g, half)
         + jnp.where(g > half, 1, 0)
         + jnp.where((g >= half) & (g < outer - 1), 1, 0)
@@ -235,7 +233,7 @@
             src_ref=sbuf.at[to],
             dst_ref=abuf.at[l],
             send_sem=a_send,
-            recv_sem=a_recv,
+            recv_sem=a_recv.at[l],
             device_id={"ctx": g * GROUP + to},
             device_id_type=MESH,
         )
@@ -260,20 +258,19 @@
         signal_of(k + 1)
         return carry
 
-    lax.fori_loop(0, ANSWER_AT, early_step, 0)
-
-    @pl.when(greetings > 0)
-    def _():
-        pl.semaphore_wait(bar, greetings)
-
-    for k in range(1, GROUP):
-        mate = lax.rem(l + k, GROUP)
-
-        @pl.when(earlier_mates(mate) < earlier_mates(l))
-        def _():
-            pl.semaphore_signal(
-                mates_in, inc=1, device_id={"ctx": g * GROUP + mate}, device_id_type=MESH
-            )
+    def send_step(k, carry):
+        first_send(k).start()
+        return carry
+
+    def state_and_send(k, carry):
+        state_of(k)
+        first_send(k).start()
+        signal_of(k + 1)
+        return carry
+
+    answer_at = LAST_ANSWER_AT - ANSWER_LESS * order
+    lax.fori_loop(0, answer_at, early_step, 0)
+    pl.semaphore_wait(bar, greetings)
 
     def tell_group(other, k):
         pl.semaphore_signal(
@@ -290,19 +287,8 @@
     def _():
         tell_group(g - 1, 2)
 
-    lax.fori_loop(ANSWER_AT, GROUP - 2, early_step, 0)
-    answers = GROUP - 1 - earlier_mates(l)
-
-    @pl.when(answers > 0)
-    def _():
-        pl.semaphore_wait(mates_in, answers)
-
-
-    def first_send_step(k, carry):
-        first_send(k).start()
-        return carry
-
-    lax.fori_loop(0, GROUP - 2, first_send_step, 0)
+    lax.fori_loop(0, answer_at, send_step, 0)
+    lax.fori_loop(answer_at, GROUP - 2, state_and_send, 0)
     state_of(GROUP - 2)
     first_send(GROUP - 2).start()
     signal_of(GROUP - 1)
@@ -327,7 +313,7 @@
         ).astype(BF16)
         return carry
 
-    lax.fori_loop(0, GROUP, gate_step, 0)
+    lax.fori_loop(0, GROUP, gate_step, 0, unroll=4)
     halo = halo_send(edges_out, edges_in, 0)
     gate_halo = halo_send(gate_edges_out, gate_edges_in, 1)
 
@@ -379,7 +365,8 @@
             inner[c, m] = weight[m] * factor[m] * begin
         return carry
 
-    early_tiles = tiles - LATE_TILES * (earlier_mates(l) // 2)
+    early_tiles = EARLY_TILES - EARLY_LESS * order
+    middle_tiles = jnp.minimum(tiles, early_tiles + jnp.where(g < half, FEW_MIDDLE, MIDDLE_TILES))
     lax.fori_loop(0, early_tiles, own_step, 0)
 
     @pl.when((l == GROUP - 1) & (g < outer - 1))
@@ -418,12 +405,19 @@
     to_first = power(rows - 1)
     to_second = power(rows - 2)
     others = pl.ds(0, GROUP - 1)
-    pltpu.make_async_copy(sbuf.at[others], abuf.at[others], a_recv).wait()
-    total, first_edge = unpack(abuf[0])
+
+    def arrived(k):
+        @pl.when(l != k)
+        def _():
+            pltpu.make_async_copy(sbuf.at[k], abuf.at[k], a_recv.at[k]).wait()
+
+        return unpack(abuf[k])
+
+    total, first_edge = arrived(0)
     first_body = total
     before = first_edge
     for k in range(1, GROUP):
-        body, edge = unpack(abuf[k])
+        body, edge = arrived(k)
         body = with_edge(body, to_first, to_second, edge, before)
         for h in range(halves):
             full[k, h * modes : h * modes + modes, :] = body[h]
@@ -456,6 +450,8 @@
     for k in range(1, outer):
         group_send(k)
 
+    lax.fori_loop(early_tiles, middle_tiles, own_step, 0)
+
     one_up = power(-1)
     two_up = power(-2)
 
@@ -475,19 +471,28 @@
     group_decay = power(rows * GROUP)
     group_first = power(rows * GROUP - 1)
     group_second = power(rows * GROUP - 2)
-    for k in range(1, outer):
-
-        @pl.when(k <= g)
-        def _():
-            pltpu.make_async_copy(tbuf, bbuf.at[k - 1], b_recv.at[k - 1]).wait()
-
     held = [jnp.zeros((modes, LANES), F32)] * halves
     before = [jnp.zeros((SUB, LANES), F32)] * halves
     for k in range(outer - 1, 0, -1):
+
+        @pl.when(k <= g)
+        def _():
+            pltpu.make_async_copy(tbuf, bbuf.at[k - 1], b_recv.at[k - 1]).wait()
+
         body, edge = unpack(bbuf[k - 1])
         body = with_edge(body, group_first, group_second, edge, before)
         held = [h * d + b for h, d, b in zip(held, group_decay, body)]
         before = edge
+    def last_send(k):
+        return pltpu.make_async_remote_copy(
+            src_ref=hbuf.at[k],
+            dst_ref=cbuf.at[l],
+            send_sem=c_send,
+            recv_sem=c_recv.at[l],
+            device_id={"ctx": g * GROUP + k},
+            device_id_type=MESH,
+        )
+
     extra[0] = jnp.concatenate(boost(first_edge, before), axis=0)
     for k in range(GROUP):
         if k == 1:
@@ -498,25 +503,13 @@
             held = [h * d + b for h, d, b in zip(held, chunk_decay, body)]
         hbuf[k] = (jnp.concatenate(held, axis=0) + extra[k]).astype(BF16)
 
-    def last_send(k):
-        to = member(k)
-        return pltpu.make_async_remote_copy(
-            src_ref=hbuf.at[to],
-            dst_ref=cbuf.at[l],
-            send_sem=c_send,
-            recv_sem=c_recv.at[l],
-            device_id={"ctx": g * GROUP + to},
-            device_id_type=MESH,
-        )
-
-    def last_send_step(k, carry):
-        last_send(k).start()
-        return carry
-
-    lax.fori_loop(0, GROUP - 1, last_send_step, 0)
+        @pl.when(l != k)
+        def _():
+            last_send(k).start()
+
     cbuf[l] = hbuf[l]
     back = scatter_rows(rows)
-    lax.fori_loop(early_tiles, tiles, own_step, 0)
+    lax.fori_loop(middle_tiles, tiles, own_step, 0)
 
     @pl.when(me > 0)
     def _():
@@ -674,11 +667,10 @@
             dma((5,)),
             dma((GROUP,)),
             dma((4,)),
-            pltpu.SemaphoreType.REGULAR,
             pltpu.SemaphoreType.REGULAR((outer - 1,)),
             pltpu.SemaphoreType.REGULAR,
             dma,
-            dma,
+            dma((GROUP,)),
             dma((outer - 1,)),
             dma((outer - 1,)),
             dma,

time: 20.6 us -> 18.6 us (0.903)
  the two profiles are of different devices: /device:TPU:240 before, /device:TPU:209 now
where the time goes in v3:
time: 18.6 us; the launch traced here: 18.5 us
  Pallas kernels  17.7 us (95%)
  local copies, waits for them, and re-layouts  0.8 us (4%)
    pallas_call x1, Pallas kernels, local(): pl.pallas_call(kernel, out_shape=pltpu.VMEM((rows, width), BF16), in_spec...  17.7 us
    unnamed x1, local copies, waits for them, and re-layouts  0.8 us

profile of v3, /device:TPU:209, one launch (start us, length us, event | category | flops | bytes accessed | tf_op | source)
XLA Modules:
  0.0 18.5 jit_solution(14246951619973503707)
XLA Ops:
  0.0 17.7 %mixer.1 = bf16[128,2048]{1,0:T(8,128)(2,1)S(1)} custom-call(bf16[3,128,2048]{2,1,0:T(8,128)(2,1)} %streams_hbm.1, f32[3,3,2048]{2,1,0:T(4,128)} %taps_hbm.1, f32[16,2048]{1,0:T(8,128)} %rates_hbm.1, f32[16,2048]{1,0:T(8,128)} %residues_hbm.1, f32[1,2048]{1,0:T(1,128)} %bitcast.1), custom_call_target="tpu_custom_call" | custom-call | tf_op jit(solution)/shard_map/mixer/pallas_call | solution.py:635
  17.7 0.8 %copy.7 = bf16[128,2048]{1,0:T(8,128)(2,1)} copy(bf16[128,2048]{1,0:T(8,128)(2,1)S(1)} %mixer.1) | data formatting | bytes 1048576

commit v4 on v3

--- a/solution.py
+++ b/solution.py
@@ -9,9 +9,9 @@
 LANES = 128
 LAST_ANSWER_AT = 6
 ANSWER_LESS = 2
-EARLY_TILES = 10
+EARLY_TILES = 9
 EARLY_LESS = 3
-MIDDLE_TILES = 4
+MIDDLE_TILES = 6
 FEW_MIDDLE = 0
 SUB = 8
 GROUP = 8
@@ -127,12 +127,24 @@
     chip = l // 2
     core = l - chip * 2
 
-    order = chip + chip // 2 - 2 * (chip // 3)
+    def chip_at(place):
+        return place + place // 2 - 2 * (place // 3)
+
+    order = chip_at(chip)
 
     def member(k):
         pair = k // 2
-        hop = 2 - pair + 3 * (pair // 2) - 2 * (pair // 3)
-        return 2 * lax.rem(chip + hop, CHIPS) + lax.rem(core + 1 + k, 2)
+        down = CHIPS - 1 - pair
+        place = down - jnp.where(down <= order, 1, 0)
+        place = jnp.where(order == CHIPS - 1, jnp.where(pair == 0, 0, down), place)
+        other = jnp.where(pair == CHIPS - 1, chip, chip_at(place))
+        return 2 * other + lax.rem(core + 1 + k, 2)
+
+    def mix_member(n):
+        up = jnp.maximum(n - 2, 0) // 2
+        place = up + jnp.where(up >= order, 1, 0)
+        other = jnp.where(n < 2, chip, chip_at(place))
+        return 2 * other + lax.rem(core + n, 2)
 
     taps_load = pltpu.make_async_copy(taps_hbm, taps, load_sem.at[0])
     rates_load = pltpu.make_async_copy(rates_hbm, rates, load_sem.at[1])
@@ -195,11 +207,12 @@
     def signal_of(k):
         p = member(k)
         at = lanes(p, piece)
-        piece_load(k).wait()
         one, one_edge = featurize(perm, streams, taps, 1, at)
         two, two_edge = featurize(perm, streams, taps, 2, at)
-        row = lax.broadcasted_iota(jnp.int32, (rows, piece), 0)
-        sig[:, at] = jnp.where((row == 0) | (row == SUB), 0.0, one * two)
+        product = one * two
+        row = lax.broadcasted_iota(jnp.int32, (2 * SUB, piece), 0)
+        sig[0 : 2 * SUB, at] = jnp.where((row == 0) | (row == SUB), 0.0, product[: 2 * SUB])
+        sig[2 * SUB :, at] = product[2 * SUB :]
         edge_row = lax.broadcasted_iota(jnp.int32, (SUB, piece), 0)
         edges = jnp.where(edge_row < 4, one_edge, two_edge)
         edges = jnp.concatenate(
@@ -249,11 +262,13 @@
         )
 
     taps_load.wait()
+    piece_load(0).wait()
     signal_of(0)
     rates_load.wait()
     decay[...] = jnp.exp(-rates[...])
 
     def early_step(k, carry):
+        piece_load(k + 1).wait()
         state_of(k)
         signal_of(k + 1)
         return carry
@@ -263,9 +278,10 @@
         return carry
 
     def state_and_send(k, carry):
+        piece_load(k + 1).wait()
         state_of(k)
+        signal_of(k + 1)
         first_send(k).start()
-        signal_of(k + 1)
         return carry
 
     answer_at = LAST_ANSWER_AT - ANSWER_LESS * order
@@ -291,6 +307,7 @@
     lax.fori_loop(answer_at, GROUP - 2, state_and_send, 0)
     state_of(GROUP - 2)
     first_send(GROUP - 2).start()
+    piece_load(GROUP - 1).wait()
     signal_of(GROUP - 1)
     state_of(GROUP - 1)
     abuf[l] = sbuf[l]
@@ -573,9 +590,10 @@
             ]
             column = []
             for b in range(steps):
-                terms = base[SUB * b : SUB * b + SUB, at]
-                for h in term:
-                    terms = terms + h
+                sums = list(term)
+                while len(sums) > 1:
+                    sums = [x + y for x, y in zip(sums[::2], sums[1::2])]
+                terms = base[SUB * b : SUB * b + SUB, at] + sums[0]
                 column.append(gate[SUB * b : SUB * b + SUB, at] * terms)
                 if b < steps - 1:
                     term = [h * f for h, f in zip(term, factor)]
@@ -588,22 +606,22 @@
             back, ready[...], preferred_element_type=F32
         ).astype(BF16)
 
-    def mix_next(k, ready, last_ready):
-        p = member(k)
+    def mix_next(n, ready, last_ready):
+        p = mix_member(n)
         pltpu.make_async_copy(hbuf.at[p], cbuf.at[p], c_recv.at[p]).wait()
-        put_back(member(k + 1), last_ready)
+        put_back(mix_member(n - 1), last_ready)
         mix_of(p, ready)
 
     mix_of(l, ready_a)
 
     def mix_pair(j, carry):
-        mix_next(GROUP - 2 - 2 * j, ready_b, ready_a)
-        mix_next(GROUP - 3 - 2 * j, ready_a, ready_b)
+        mix_next(2 * j + 1, ready_b, ready_a)
+        mix_next(2 * j + 2, ready_a, ready_b)
         return carry
 
     lax.fori_loop(0, GROUP // 2 - 1, mix_pair, 0)
-    mix_next(0, ready_b, ready_a)
-    put_back(member(0), ready_b)
+    mix_next(GROUP - 1, ready_b, ready_a)
+    put_back(mix_member(GROUP - 1), ready_b)
 
     @pl.when(me < count - 1)
     def _():

time: 18.6 us -> 17.6 us (0.946)
  Pallas kernels: 17.7 us -> 16.7 us
    pallas_call x1, Pallas kernels: 17.7 us -> 16.7 us  [local(): pl.pallas_call(kernel, out_shape=pltpu.VMEM((rows, width), BF16), in_spec...]
where the time goes in v4:
time: 17.6 us; the launch traced here: 17.5 us
  Pallas kernels  16.7 us (95%)
  local copies, waits for them, and re-layouts  0.8 us (5%)
    pallas_call x1, Pallas kernels, local(): pl.pallas_call(kernel, out_shape=pltpu.VMEM((rows, width), BF16), in_spec...  16.7 us
    unnamed x1, local copies, waits for them, and re-layouts  0.8 us

profile of v4, /device:TPU:209, one launch (start us, length us, event | category | flops | bytes accessed | tf_op | source)
XLA Modules:
  0.0 17.5 jit_solution(13690550055373105148)
XLA Ops:
  0.0 16.7 %mixer.1 = bf16[128,2048]{1,0:T(8,128)(2,1)S(1)} custom-call(bf16[3,128,2048]{2,1,0:T(8,128)(2,1)} %streams_hbm.1, f32[3,3,2048]{2,1,0:T(4,128)} %taps_hbm.1, f32[16,2048]{1,0:T(8,128)} %rates_hbm.1, f32[16,2048]{1,0:T(8,128)} %residues_hbm.1, f32[1,2048]{1,0:T(1,128)} %bitcast.1), custom_call_target="tpu_custom_call" | custom-call | tf_op jit(solution)/shard_map/mixer/pallas_call | solution.py:653
  16.7 0.8 %copy.7 = bf16[128,2048]{1,0:T(8,128)(2,1)} copy(bf16[128,2048]{1,0:T(8,128)(2,1)S(1)} %mixer.1) | data formatting | bytes 1048576

commit v5 on v4

--- a/solution.py
+++ b/solution.py
@@ -60,6 +60,21 @@
 def edge_signal(weights, own, before):
     features = edge_features(weights, own, before)
     return features * pltpu.roll(features, 4, 0)
+
+
+def row_sums(values, row):
+    def first(a, b):
+        top = row < 4
+        return jnp.where(top, a, b) + pltpu.roll(jnp.where(top, b, a), 4, 0)
+
+    def merge(a, b, step):
+        return jnp.where(
+            (row & step) != 0, a + pltpu.roll(a, step, 0), b + pltpu.roll(b, SUB - step, 0)
+        )
+
+    odd = merge(first(values[3], values[7]), first(values[1], values[5]), 2)
+    even = merge(first(values[2], values[6]), first(values[0], values[4]), 2)
+    return merge(odd, even, 1)
 
 
 def edge_weights(taps, at):
@@ -235,9 +250,9 @@
             ends = []
             for m in range(modes):
                 weight = jnp.exp(to_end * rates[pl.ds(m, 1), at])
-                ends.append(jnp.sum(held[m] * weight, axis=0, keepdims=True))
+                ends.append(held[m] * weight)
             sbuf[p, half * modes : half * modes + modes, :] = jnp.concatenate(
-                ends, axis=0
+                [row_sums(ends[m : m + SUB], sub_row) for m in range(0, modes, SUB)], axis=0
             ).astype(BF16)
 
     def first_send(k):

time: 17.6 us -> 17.5 us (level)
  no operation moved by 1% of the time
where the time goes in v5:
time: 17.5 us; the launch traced here: 17.4 us
  Pallas kernels  16.6 us (95%)
  local copies, waits for them, and re-layouts  0.8 us (5%)
    pallas_call x1, Pallas kernels, local(): pl.pallas_call(kernel, out_shape=pltpu.VMEM((rows, width), BF16), in_spec...  16.6 us
    unnamed x1, local copies, waits for them, and re-layouts  0.8 us

profile of v5, /device:TPU:209, one launch (start us, length us, event | category | flops | bytes accessed | tf_op | source)
XLA Modules:
  0.0 17.4 jit_solution(2355371442875701203)
XLA Ops:
  0.0 16.6 %mixer.1 = bf16[128,2048]{1,0:T(8,128)(2,1)S(1)} custom-call(bf16[3,128,2048]{2,1,0:T(8,128)(2,1)} %streams_hbm.1, f32[3,3,2048]{2,1,0:T(4,128)} %taps_hbm.1, f32[16,2048]{1,0:T(8,128)} %rates_hbm.1, f32[16,2048]{1,0:T(8,128)} %residues_hbm.1, f32[1,2048]{1,0:T(1,128)} %bitcast.1), custom_call_target="tpu_custom_call" | custom-call | tf_op jit(solution)/shard_map/mixer/pallas_call | solution.py:668
  16.6 0.8 %copy.7 = bf16[128,2048]{1,0:T(8,128)(2,1)} copy(bf16[128,2048]{1,0:T(8,128)(2,1)S(1)} %mixer.1) | data formatting | bytes 1048576
